TPU v7x, 512 devices: a whole 4x4x16 slice. The times are simulated.
512 devices in a mesh: tm: 16 (over z_lo, core), space: 32 (over x, y, z_hi).
Axes of the slice: x: 4, y: 4, z: 16 (z_hi: 2, z_lo: 8; z = z_hi * 8 + z_lo), core: 2. Of those that a mesh axis runs over, the one named last changes fastest.
Arguments:
- slab_queue: bfloat16 [2, 16, 512, 3072], P(None, 'tm', 'space'), may hold values from -6 to 6
- levels: int32 [2, 16], replicated, may hold values from 0 to 47, as said below
- mod_table: bfloat16 [48, 3, 3072], replicated, may hold values from -3 to 3
- w_qkv: bfloat16 [3072, 16, 384], P(None, 'tm'), may hold values from -0.109375 to 0.109375
- q_gain: float32 [16, 128], P('tm'), may hold values from 0.5 to 12
- k_gain: float32 [16, 128], P('tm'), may hold values from 0.5 to 12
- w_out: bfloat16 [2048, 3072], P('tm'), may hold values from -0.125 to 0.125
Outputs:
- advanced: bfloat16 [2, 16, 512, 3072], P(None, 'tm', 'space')
Inputs may be any that keep to these rules, and one draw needn't show every extreme that they name: `levels`: the level of slab s lies from s * 3 up to, not including, (s + 1) * 3.
All inputs are finite; a program needn't handle non-finite values.
Results may differ from a plain program's by a relative error of at most 0.015.
Values may be sent and summed in bfloat16 or wider, within the bound.
A program may use at most 64 MiB of HBM per device.

v0:
```python
import functools
import math

import jax
import jax.numpy as jnp
from jax import lax
from jax.experimental import pallas as pl
from jax.experimental.pallas import tpu as pltpu
from jax.sharding import PartitionSpec as P

HEAD_DIM = 128
W_PIECES = 12
RING_PARTS = 2
SUM_PIECES = 4
SUM_PARTS = 2
VMEM_BYTES = 63 * 1024 * 1024
MESH = pl.DeviceIdType.MESH
F32 = jnp.float32
BF16 = jnp.bfloat16


def dot_t(left, right):
    return lax.dot_general(left, right, (((1,), (1,)), ((), ())), preferred_element_type=F32)


def head_norm(values, gain):
    values = values.astype(F32)
    factor = lax.rsqrt(jnp.mean(jnp.square(values), axis=-1, keepdims=True) + 1e-06)
    return (values * factor * gain).astype(BF16)


def kernel(
    ring, cols,
    slab_in, levels_in, mod_in, w_qkv, q_gain, k_gain, w_out,
    out,
    slab, levels, mod, rows_of, mod_send, tokens, w_buf, gq, gk, wo, qkv, sp_in, sp_out, sp_back, tmp_out, comb,
    x_send, x_recv, part, r_send, r_recv, l_send, l_recv, r_last, l_last, prev, fin_send, fin_recv,
    loc_sem, pair_send, pair_recv, ag_send, ag_recv, aa_send, aa_recv, rt_send, rt_recv,
    xs_send, xs_recv, rs_send, rs_recv, last_recv, misc_send, misc_recv, w_send, w_recv,
    wz_send, wz_recv, wp_send, wp_recv, wd_sem,
):
    half = ring // 2
    group = 2 if ring > 4 else 1
    stride = half // group
    peers = ring // stride
    pieces = stride // 2
    slabs = ring
    tok, width = slab.shape[1], slab.shape[2]
    piece = width // W_PIECES
    tm, space = lax.axis_index("tm"), lax.axis_index("space")
    core, z_lo = lax.rem(tm, 2), lax.div(tm, 2)
    me, z_hi = lax.div(space, 2), lax.rem(space, 2)
    z = z_hi * half + z_lo
    other = 1 - core
    inv_root = 1.0 / math.sqrt(HEAD_DIM)

    def mod_ring(value):
        return lax.rem(value + ring, ring)

    def device(plane, of_core, column):
        return (lax.rem(plane, half) * 2 + of_core, column * 2 + lax.div(plane, half))

    def here(column):
        return (tm, column * 2 + z_hi)

    right = device(mod_ring(z + 1), core, me)
    left = device(mod_ring(z - 1), core, me)
    partner = (z_lo * 2 + other, space)
    tm_next = (lax.rem(tm + 1, slabs), space)
    tm_far = (lax.rem(tm + jnp.where(core == 1, 1, slabs - 1), slabs), space)

    def remote(src, dst, send_sem, recv_sem, target):
        return pltpu.make_async_remote_copy(
            src_ref=src, dst_ref=dst, send_sem=send_sem, recv_sem=recv_sem,
            device_id=target, device_id_type=MESH,
        )

    own_head = core == z_hi
    fetch_levels = pltpu.make_async_copy(levels_in, levels, loc_sem.at[2])
    fetch_mod = pltpu.make_async_copy(mod_in, mod, loc_sem.at[3])
    fetch_slab = pltpu.make_async_copy(slab_in, slab, loc_sem.at[4])
    local_w = pltpu.make_async_copy(w_qkv, w_buf, loc_sem.at[0])
    local_wo = pltpu.make_async_copy(w_out, wo.at[0, core], loc_sem.at[1])
    local_gq = pltpu.make_async_copy(q_gain, gq, loc_sem.at[5])
    local_gk = pltpu.make_async_copy(k_gain, gk, loc_sem.at[6])
    fetch_levels.start()
    fetch_mod.start()
    fetch_slab.start()

    barrier = pltpu.get_barrier_semaphore()
    right_of = [device(mod_ring(z + 1), at, me) for at in (0, 1)]
    left_of = [device(mod_ring(z - 1), at, me) for at in (0, 1)]
    for target in (*right_of, *left_of, partner, tm_far):
        pl.semaphore_signal(barrier, inc=1, device_id=target, device_id_type=MESH)

    def greet(step, carry):
        column = lax.rem(me + step, cols)
        pl.semaphore_signal(barrier, inc=1, device_id=here(column), device_id_type=MESH)
        return carry

    lax.fori_loop(1, cols, greet, 0)

    def greet_class(step, carry):
        target = device(mod_ring(z + stride * step), core, me)
        pl.semaphore_signal(barrier, inc=1, device_id=target, device_id_type=MESH)
        return carry

    lax.fori_loop(1, peers, greet_class, 0)

    fetch_levels.wait()
    fetch_mod.wait()

    tm_before = lax.rem(tm + slabs - 1, slabs)
    pick_row = lax.broadcasted_iota(jnp.int32, (16, mod.shape[1]), 0)
    pick_col = lax.broadcasted_iota(jnp.int32, (16, mod.shape[1]), 1)
    hot = jnp.zeros((16, mod.shape[1]), F32)
    for at, (batch, of_slab) in enumerate(((0, tm), (1, tm), (0, tm_before), (1, tm_before))):
        hot = jnp.where((pick_row == at) & (pick_col == levels[batch, of_slab]), 1.0, hot)
    for kind in range(3):
        picked = jnp.dot(hot.astype(BF16), mod[kind], preferred_element_type=F32)
        for at in range(4):
            rows_of[kind, at] = picked[at : at + 1]

    def modulate(batch):
        values = slab[batch].astype(F32)
        centre = jnp.mean(values, axis=-1, keepdims=True)
        moved = values - centre
        spread = jnp.mean(jnp.square(moved), axis=-1, keepdims=True)
        normed = moved * lax.rsqrt(spread + 1e-06)
        return (normed * (1.0 + rows_of[1, batch]) + rows_of[0, batch]).astype(BF16)

    fetch_slab.wait()

    @pl.when(own_head)
    def _():
        local_gq.start()
        local_gk.start()
        local_w.start()

    local_wo.start()

    tokens[z * 2 + core] = modulate(core)
    pl.semaphore_wait(barrier, 6 + cols - 1 + peers - 1)

    span = width // RING_PARTS

    def gather_copy(way, step, t, origin, at):
        block = tokens.at[origin * 2 + t, :, at * span : (at + 1) * span]
        return remote(
            block, block, ag_send.at[0], ag_recv.at[way, step, t, at], (right, left)[way]
        )

    def gather_start(t):
        for at in range(RING_PARTS):
            for way in (0, 1):
                gather_copy(way, 1, t, z, at).start()

    gather_start(core)
    mod_send[...] = modulate(other)
    to_pair = remote(mod_send, tokens.at[z * 2 + core], pair_send.at[0], pair_recv.at[0], partner)
    to_pair.start()
    from_pair = remote(mod_send, tokens.at[z * 2 + other], pair_send.at[0], pair_recv.at[0], partner)
    from_pair.wait_recv()
    gather_start(other)

    def give_w(at):
        rows = pl.ds(at * piece, piece)
        return remote(w_qkv.at[rows], w_buf.at[rows], w_send.at[0], w_recv.at[0], partner)

    whole_w = remote(w_qkv, w_buf, w_send.at[0], w_recv.at[0], partner)
    give_gq = remote(q_gain, gq, pair_send.at[2], pair_recv.at[2], partner)
    give_gk = remote(k_gain, gk, pair_send.at[3], pair_recv.at[3], partner)
    give_wo = remote(w_out, wo.at[0, core], pair_send.at[4], pair_recv.at[4], partner)
    take_wo = remote(w_out, wo.at[0, other], pair_send.at[4], pair_recv.at[4], partner)
    pass_slab = remote(slab, prev, misc_send.at[0], misc_recv.at[0], tm_next)

    @pl.when(own_head)
    def _():
        give_gq.start()
        give_gk.start()

    pairs = group
    rows_w = 2 * HEAD_DIM // cols
    cut_rows = pl.ds(pl.multiple_of(lax.div(me, 2) * rows_w, rows_w), rows_w)
    cut_cols = pl.ds(pl.multiple_of(lax.rem(me, 2) * (width // 2), width // 2), width // 2)

    def plane_piece(at):
        apart = stride * at if 2 * stride * at < half else stride * at - half
        if 2 * stride * at == half:
            apart = jnp.where(core == 0, half // 2, -(half // 2))
        return remote(
            w_out.at[cut_rows, cut_cols], wo.at[at, core, cut_rows, cut_cols],
            wz_send.at[at], wz_recv.at[at], device(mod_ring(z - apart), core, me),
        )

    def spread_piece(column, source):
        rows = pl.ds(pl.multiple_of(lax.div(source, 2) * rows_w, rows_w), rows_w)
        span = pl.ds(pl.multiple_of(lax.rem(source, 2) * (width // 2), width // 2), width // 2)
        piece_of = wo.at[1:pairs, core, rows, span]
        return remote(
            piece_of, piece_of, wp_send.at[column], wp_recv.at[source], here(column)
        )

    def pair_wo(of_core):
        block = wo.at[1:pairs, of_core]
        return remote(block, block, wd_sem.at[0], wd_sem.at[1], partner)

    for at in range(1, pairs):
        plane_piece(at).start()

    def slab_copy(hi, column, source):
        return remote(
            qkv.at[hi, column], sp_in.at[source, hi], aa_send.at[0], aa_recv.at[0],
            here(column),
        )

    first_dot = max(1, 3 * half // 8)
    give_steps = max(first_dot - 1, 1)
    per_step = W_PIECES // give_steps

    def reach(at):
        done = jnp.minimum(2 * (at - first_dot + 1), at + 1)
        return jnp.where(at < first_dot, 0, jnp.where(at == half, half + 1, done))

    def gather_step(step, carry):
        step = jnp.asarray(step, jnp.int32)
        plane_a = mod_ring(z - step)
        plane_b = mod_ring(z + step)
        first, last = reach(step - 1), reach(step)
        middle = jnp.where(last - first == 2, first + 1, first)

        def turn_step(turn, inner):
            t = jnp.where(turn == 0, core, other)
            for at in range(RING_PARTS):
                for way, origin in ((0, plane_a), (1, plane_b)):

                    @pl.when((step < half) | (t == way))
                    def _():
                        gather_copy(way, step, t, origin, at).wait_recv()

                    @pl.when((step < half - 1) | ((step == half - 1) & (t == way)))
                    def _():
                        gather_copy(way, step + 1, t, origin, at).start()

            if pairs > 1:

                @pl.when((step == 2) & (turn == 0))
                def _():
                    for at in range(1, pairs):
                        plane_piece(at).wait_recv()

                    def spread(ahead, most):
                        spread_piece(lax.rem(me + ahead, cols), me).start()
                        return most

                    lax.fori_loop(1, cols, spread, 0)

                @pl.when((step == half - 1) & (turn == 0))
                def _():
                    def await_spread(ahead, most):
                        spread_piece(me, lax.rem(me + ahead, cols)).wait_recv()
                        return most

                    lax.fori_loop(1, cols, await_spread, 0)
                    pair_wo(core).start()

            @pl.when(own_head & (step <= give_steps))
            def _():
                def one(at, most):
                    give_w(at).start()
                    return most

                share = per_step // 2
                begin = (2 * (step - 1) + turn) * share
                lax.fori_loop(begin, begin + share, one, 0)

            @pl.when((step == first_dot) & (turn == 0))
            def _():
                give_wo.start()

                @pl.when(own_head)
                def _():
                    local_w.wait()
                    local_gq.wait()
                    local_gk.wait()

                @pl.when(jnp.logical_not(own_head))
                def _():
                    whole_w.wait_recv()
                    give_gq.wait_recv()
                    give_gk.wait_recv()

            lax.fori_loop(
                jnp.where(turn == 0, first, middle), jnp.where(turn == 0, middle, last),
                project_step, 0,
            )
            return inner

        lax.fori_loop(0, 2, turn_step, 0)
        return carry

    def project_step(step, carry):
        planes = (mod_ring(z - step), mod_ring(z + step))
        rows = jnp.concatenate(
            [tokens[pl.ds(plane * 2, 2)].reshape(2 * tok, width) for plane in planes], axis=0
        )
        projected = jnp.dot(rows, w_buf[...], preferred_element_type=F32).astype(BF16)
        queries = head_norm(projected[:, :HEAD_DIM], gq[...])
        keys = head_norm(projected[:, HEAD_DIM : 2 * HEAD_DIM], gk[...])
        values = projected[:, 2 * HEAD_DIM :]
        def place(at):
            hi, lo = lax.div(planes[at], half), lax.rem(planes[at], half)
            for t in (0, 1):
                cut = slice((at * 2 + t) * tok, (at * 2 + t + 1) * tok)
                column = lo * 2 + t
                qkv[hi, column, :, 0:HEAD_DIM] = queries[cut]
                qkv[hi, column, :, HEAD_DIM : 2 * HEAD_DIM] = keys[cut]
                qkv[hi, column, :, 2 * HEAD_DIM :] = values[cut]

                @pl.when(column != me)
                def _():
                    slab_copy(hi, column, me).start()

        place(0)

        @pl.when(lax.rem(step, half) != 0)
        def _():
            place(1)

        return carry

    rows_t = slabs * tok
    at_row = lax.broadcasted_iota(jnp.int32, (rows_t, rows_t), 0) & (tok - 1)
    at_col = lax.broadcasted_iota(jnp.int32, (rows_t, rows_t), 1) & (tok - 1)
    same = at_row == at_col

    def temporal(hi):
        queries = qkv[hi, :, :, 0:HEAD_DIM].reshape(rows_t, HEAD_DIM)
        keys = qkv[hi, :, :, HEAD_DIM : 2 * HEAD_DIM].reshape(rows_t, HEAD_DIM)
        values = qkv[hi, :, :, 2 * HEAD_DIM :].reshape(rows_t, HEAD_DIM)
        scores = jnp.where(same, dot_t(queries, keys) * inv_root, -jnp.inf)
        weights = jnp.exp(scores - jnp.max(scores, axis=-1, keepdims=True))
        total = jnp.sum(weights, axis=-1, keepdims=True)
        mixed = jnp.dot(weights.astype(BF16), values, preferred_element_type=F32) / total
        tmp_out[hi] = mixed.reshape(slabs, tok, HEAD_DIM)

    lax.fori_loop(1, half, gather_step, 0)
    temporal(z_hi)
    gather_step(half, 0)
    pass_slab.start()
    sp_in[me] = qkv[:, me]

    mine_late = lax.div(me, 2) == z_lo

    @pl.when(mine_late)
    def _():
        temporal(1 - z_hi)

    part_in = sp_in.at[0 : cols - 1]
    remote(part_in, part_in, aa_send.at[0], aa_recv.at[0], partner).wait_recv()

    is_late = jnp.where(mine_late, 1, 0)

    def back_copy(column, of_slab):
        return remote(
            sp_out.at[column], sp_back.at[:, of_slab], rt_send.at[0], rt_recv.at[is_late],
            here(column),
        )

    batch_s = min(8, cols)
    rows_s = batch_s * 2 * tok

    def spatial_step(step, carry):
        keys = sp_in[:, :, :, HEAD_DIM : 2 * HEAD_DIM].reshape(cols * 2 * tok, HEAD_DIM)
        values = sp_in[:, :, :, 2 * HEAD_DIM :].reshape(cols * 2 * tok, HEAD_DIM)
        queries = sp_in[pl.ds(step * batch_s, batch_s), :, :, 0:HEAD_DIM].reshape(rows_s, HEAD_DIM)
        scores = dot_t(queries, keys) * inv_root
        weights = jnp.exp(scores - jnp.max(scores, axis=-1, keepdims=True))
        total = jnp.sum(weights, axis=-1, keepdims=True)
        mixed = jnp.dot(weights.astype(BF16), values, preferred_element_type=F32) / total
        sp_out[pl.ds(step * batch_s, batch_s)] = mixed.astype(BF16).reshape(batch_s, 2, tok, HEAD_DIM)
        for at in range(batch_s):
            column = step * batch_s + at

            @pl.when(column != me)
            def _():
                back_copy(column, me).start()

        return carry

    lax.fori_loop(0, cols // batch_s, spatial_step, 0)
    sp_back[:, me] = sp_out[me]

    @pl.when(jnp.logical_not(mine_late))
    def _():
        temporal(1 - z_hi)


    def await_back(late, count):
        block = sp_back.at[:, 0:count]
        remote(block, block, rt_send.at[0], rt_recv.at[late], partner).wait_recv()

    def combine(ahead, carry):
        of_slab = lax.rem(2 * z_lo + ahead, slabs)
        both = sp_back[:, of_slab].astype(F32) + tmp_out[:, of_slab]
        comb[:, of_slab] = both.astype(BF16)
        return carry

    @pl.when(mine_late)
    def _():
        await_back(0, slabs - 2)

    @pl.when(jnp.logical_not(mine_late))
    def _():
        await_back(0, slabs - 3)

    lax.fori_loop(2, slabs, combine, 0)

    def fill(dst, plane, piece_at):
        def one(at, carry):
            step = lax.div(at, 2)
            block = jnp.where(lax.rem(at, 2) == 0, 2 * stride - 1 - step, step)
            place = lax.rem(2 * plane + 2 * ring - (stride - 1) + block, 2 * ring)
            from_slab = lax.rem(lax.rem(place, slabs) + slabs - 1, slabs)
            dst[at] = comb[lax.div(place, slabs), from_slab]
            return carry

        lax.fori_loop(4 * piece_at, 4 * piece_at + 4, one, 0)

    def head_copy(step, at):
        plane = mod_ring(z + stride * step)
        slot = lax.div(lax.rem(z_lo - lax.rem(plane, half) + half, half), stride)
        rows = pl.ds(4 * at, 4)
        return remote(
            x_send.at[step, rows], x_recv.at[slot, z_hi, rows],
            xs_send.at[step, at], xs_recv.at[slot, z_hi, at], device(plane, core, me),
        )

    def send_heads(step, at):
        fill(x_send.at[step], mod_ring(z + stride * step), at)
        head_copy(step, at).start()

    far = peers // 2
    for at in range(pieces):
        if at < pieces - 1:
            send_heads(far, at)
        for step in range(1, peers):
            if step != far:
                send_heads(step, at)
    for at in range(pieces - 1):
        fill(x_recv.at[0, z_hi], z, at)

    @pl.when(mine_late)
    def _():
        await_back(1, 1)

    @pl.when(jnp.logical_not(mine_late))
    def _():
        await_back(1, 2)

    lax.fori_loop(0, 2, combine, 0)
    send_heads(far, pieces - 1)
    fill(x_recv.at[0, z_hi], z, pieces - 1)
    local_wo.wait()
    take_wo.wait_recv()
    if pairs > 1:
        pair_wo(other).wait_recv()

    to_pair.wait_send()

    @pl.when(own_head)
    def _():
        whole_w.wait_send()
        give_gq.wait_send()
        give_gk.wait_send()

    give_wo.wait_send()
    pass_slab.wait_send()
    pass_slab.wait_recv()
    for at in range(1, pairs):
        plane_piece(at).wait_send()
    if pairs > 1:
        pair_wo(core).wait_send()

        def drain_spread(ahead, carry):
            spread_piece(lax.rem(me + ahead, cols), me).wait_send()
            return carry

        lax.fori_loop(1, cols, drain_spread, 0)
    sent = tokens.at[0 : 2 * ring - 2]
    remote(sent, sent, ag_send.at[0], ag_recv.at[0, 0, 0, 0], partner).wait_send()
    sent = qkv.at[:, 0 : cols - 1]
    remote(sent, sent, aa_send.at[0], aa_recv.at[0], partner).wait_send()
    sent = sp_out.at[0 : cols - 1]
    remote(sent, sent, rt_send.at[0], rt_recv.at[0], partner).wait_send()

    def await_heads(at):
        for step in range(1, peers):
            plane = mod_ring(z + stride * step)
            slot = lax.div(lax.rem(lax.rem(plane, half) - z_lo + half, half), stride)
            hi = lax.div(plane, half)
            rows = pl.ds(4 * at, 4)
            remote(
                x_send.at[step, rows], x_recv.at[slot, hi, rows],
                xs_send.at[step, at], xs_recv.at[slot, hi, at], device(plane, core, me),
            ).wait_recv()

    def final_core(way, step):
        if step < stride - 3:
            return None
        return (step == stride - 3) != (way == 1) and 1 or 0

    def sum_copy(way, step, at):
        mine, theirs, ends = ((r_send, r_recv, r_last), (l_send, l_recv, l_last))[way]
        span_s = slice(at * sum_span, (at + 1) * sum_span)
        dst = theirs.at[step, :, span_s]
        sem = rs_recv.at[way, step, at]
        target = (right, left)[way]
        to_core = final_core(way, step)
        if to_core is not None:
            dst = ends.at[core, :, span_s]
            sem = last_recv.at[way, core, at]
            target = (right_of, left_of)[way][to_core]
        return remote(mine.at[step, :, span_s], dst, rs_send.at[way, step, at], sem, target)

    sum_span = width // SUM_PARTS
    chunk = width // SUM_PIECES
    rows_x = 4 * tok
    for step in range(stride - 1):
        if step % 2 == 0:
            await_heads(step // 2)
            rows = slice(2 * step, 2 * step + 4)
            heads = jnp.concatenate(
                [x_recv[at // 2, at % 2, rows].reshape(rows_x, HEAD_DIM) for at in range(2 * pairs)],
                axis=1,
            )
        for part_at in range(SUM_PARTS):
            span_s = slice(part_at * sum_span, (part_at + 1) * sum_span)
            if step % 2 == 0:
                for at in range(part_at * sum_span, (part_at + 1) * sum_span, chunk):
                    weights = wo[:, :, :, at : at + chunk].reshape(2 * pairs * HEAD_DIM, chunk)
                    product = jnp.dot(heads, weights, preferred_element_type=F32)
                    part[rows, :, at : at + chunk] = product.reshape(4, tok, chunk)
            for way, mine, theirs in ((0, r_send, r_recv), (1, l_send, l_recv)):
                share = part[step * 2 + way, :, span_s]
                if step >= 2:
                    sum_copy(way, step - 2, part_at).wait_recv()
                    share = share + theirs[step - 2, :, span_s].astype(F32)
                mine[step, :, span_s] = share.astype(BF16)
                sum_copy(way, step, part_at).start()

    fin_send[...] = part[2 * stride - 1 - other].astype(BF16)
    give_fin = remote(fin_send, fin_recv, misc_send.at[1], misc_recv.at[1], partner)
    give_fin.start()

    def drain_sum(step):
        for way in (0, 1):
            for at in range(SUM_PARTS):
                sum_copy(way, step, at).wait_send()

    for step in range(1, peers):
        for at in range(pieces):
            head_copy(step, at).wait_send()
    for step in range(stride - 2):
        drain_sum(step)

    def await_last(way, batch):
        ends = (r_last, l_last)[way]
        for at in range(SUM_PARTS):
            dst = ends.at[batch, :, at * sum_span : (at + 1) * sum_span]
            remote(
                dst, dst, rs_send.at[way, 0, at], last_recv.at[way, batch, at], partner
            ).wait_recv()

    def attend(batch, own_share):
        gate = rows_of[2, 2 + batch]
        if stride > 2:
            for way in (0, 1):
                await_last(way, batch)
            sides = r_last[batch].astype(F32) + l_last[batch].astype(F32)
        else:
            for way in (0, 1):

                @pl.when(core == way)
                def _():
                    await_last(way, batch)

            sides = jnp.where(core == 0, r_last[batch].astype(F32), l_last[batch].astype(F32))
        projection = own_share + sides
        out[batch] = (prev[batch].astype(F32) + gate * projection).astype(BF16)

    attend(core, part[2 * stride - 1 - core])
    give_fin.wait_recv()
    attend(other, fin_recv[...].astype(F32))

    give_fin.wait_send()
    drain_sum(stride - 2)


def body(slab_queue, levels, mod_table, w_qkv, q_gain, k_gain, w_out):
    batch, _, tok, width = slab_queue.shape
    ring = lax.axis_size("tm")
    cols = lax.axis_size("space") // 2
    half = ring // 2
    group = 2 if ring > 4 else 1
    stride = half // group
    vmem = pl.BlockSpec(memory_space=pltpu.VMEM)
    hbm = pl.BlockSpec(memory_space=pltpu.HBM)
    dma = pltpu.SemaphoreType.DMA
    block = (tok, width)
    return pl.pallas_call(
        functools.partial(kernel, ring, cols),
        out_shape=pltpu.VMEM((batch, tok, width), BF16),
        in_specs=[hbm] * 7,
        out_specs=vmem,
        scratch_shapes=[
            pltpu.VMEM((batch,) + block, BF16),
            pltpu.SMEM(levels.shape, jnp.int32),
            pltpu.VMEM((3, mod_table.shape[0], width), BF16),
            pltpu.VMEM((3, 4, 1, width), F32),
            pltpu.VMEM(block, BF16),
            pltpu.VMEM((2 * ring,) + block, BF16),
            pltpu.VMEM((width, 3 * HEAD_DIM), BF16),
            pltpu.VMEM((1, HEAD_DIM), F32),
            pltpu.VMEM((1, HEAD_DIM), F32),
            pltpu.VMEM((group, 2, HEAD_DIM, width), BF16),
            pltpu.VMEM((2, ring, tok, 3 * HEAD_DIM), BF16),
            pltpu.VMEM((cols, 2, tok, 3 * HEAD_DIM), BF16),
            pltpu.VMEM((cols, 2, tok, HEAD_DIM), BF16),
            pltpu.VMEM((2, ring, tok, HEAD_DIM), BF16),
            pltpu.VMEM((2, ring, tok, HEAD_DIM), F32),
            pltpu.VMEM((2, ring, tok, HEAD_DIM), BF16),
            pltpu.VMEM((ring // stride, 2 * stride, tok, HEAD_DIM), BF16),
            pltpu.VMEM((group, 2, 2 * stride, tok, HEAD_DIM), BF16),
            pltpu.VMEM((2 * stride,) + block, F32),
            pltpu.VMEM((stride - 1,) + block, BF16),
            pltpu.VMEM((stride - 1,) + block, BF16),
            pltpu.VMEM((stride - 1,) + block, BF16),
            pltpu.VMEM((stride - 1,) + block, BF16),
            pltpu.VMEM((batch,) + block, BF16),
            pltpu.VMEM((batch,) + block, BF16),
            pltpu.VMEM((batch,) + block, BF16),
            pltpu.VMEM(block, BF16),
            pltpu.VMEM(block, BF16),
            dma((7,)),
            dma((5,)),
            dma((5,)),
            dma((1,)),
            dma((2, half + 1, 2, RING_PARTS)),
            dma((1,)),
            dma((1,)),
            dma((1,)),
            dma((2,)),
            dma((ring // stride, stride // 2)),
            dma((group, 2, stride // 2)),
            dma((2, stride - 1, SUM_PARTS)),
            dma((2, stride - 1, SUM_PARTS)),
            dma((2, batch, SUM_PARTS)),
            dma((2,)),
            dma((2,)),
            dma((1,)),
            dma((1,)),
            dma((group,)),
            dma((group,)),
            dma((cols,)),
            dma((cols,)),
            dma((2,)),
        ],
        compiler_params=pltpu.CompilerParams(
            collective_id=0, has_side_effects=True, vmem_limit_bytes=VMEM_BYTES
        ),
        cost_estimate=pl.CostEstimate(
            flops=4 * 10**9, bytes_accessed=8 * 10**6, transcendentals=4 * 10**5
        ),
    )(
        slab_queue.reshape(batch, tok, width), levels, jnp.swapaxes(mod_table, 0, 1),
        w_qkv.reshape(width, 3 * HEAD_DIM), q_gain, k_gain, w_out,
    ).reshape(batch, 1, tok, width)


def solution(mesh):
    placed = (
        P(None, "tm", "space", None),
        P(),
        P(),
        P(None, "tm", None),
        P("tm", None),
        P("tm", None),
        P("tm", None),
    )
    return jax.shard_map(
        body, mesh=mesh, in_specs=placed, out_specs=P(None, "tm", "space", None), check_vma=False
    )
```

profile of v0, /device:TPU:6, one launch (start us, length us, event | category | flops | bytes accessed | tf_op | source)
XLA Modules:
  0.0 79.8 jit_solution(16476979213646815399)
XLA Ops:
  0.0 79.1 %shard_map.73 = bf16[2,16,3072]{2,1,0:T(8,128)(2,1)S(1)} custom-call(bf16[2,16,3072]{2,1,0:T(8,128)(2,1)} %bitcast.9, s32[2,16]{1,0:T(2,128)} %levels_in.1, bf16[3,48,3072]{2,1,0:T(8,128)(2,1)} %bitcast.8, bf16[3072,384]{1,0:T(8,128)(2,1)} %bitcast.7, f32[1,128]{1,0:T(1,128)} %q_gain.1, f32[1,128]{1,0:T(1,128)} %k_gain.1, bf16[128,3072]{1,0:T(8,128)(2,1)} %w_out.1), custom_call_target="tpu_custom_call" | custom-call | flops 4000000000 | bytes 8000000 | tf_op jit(solution)/shard_map/pallas_call | solution.py:611
  79.1 0.7 copy.10
where the time goes:
time: 79.9 us; the launch traced here: 79.8 us
  Pallas kernels  79.1 us (99%)
    pallas_call x1, Pallas kernels, body(): pl.pallas_call(functools.partial(kernel, ring, cols), out_shape=pltpu.VME...  79.1 us

commit v1 on v0

--- a/solution.py
+++ b/solution.py
@@ -12,7 +12,7 @@
 W_PIECES = 12
 RING_PARTS = 2
 SUM_PIECES = 4
-SUM_PARTS = 2
+SUM_PARTS = 4
 VMEM_BYTES = 63 * 1024 * 1024
 MESH = pl.DeviceIdType.MESH
 F32 = jnp.float32

time: 79.9 us -> 80.2 us (level)
  no operation moved by 1% of the time
where the time goes in v1:
time: 80.2 us; the launch traced here: 80 us
  Pallas kernels  79.3 us (99%)
    pallas_call x1, Pallas kernels, body(): pl.pallas_call(functools.partial(kernel, ring, cols), out_shape=pltpu.VME...  79.3 us

profile of v1, /device:TPU:6, one launch (start us, length us, event | category | flops | bytes accessed | tf_op | source)
XLA Modules:
  0.0 80.0 jit_solution(15723332856275492798)
XLA Ops:
  0.0 79.3 %shard_map.73 = bf16[2,16,3072]{2,1,0:T(8,128)(2,1)S(1)} custom-call(bf16[2,16,3072]{2,1,0:T(8,128)(2,1)} %bitcast.9, s32[2,16]{1,0:T(2,128)} %levels_in.1, bf16[3,48,3072]{2,1,0:T(8,128)(2,1)} %bitcast.8, bf16[3072,384]{1,0:T(8,128)(2,1)} %bitcast.7, f32[1,128]{1,0:T(1,128)} %q_gain.1, f32[1,128]{1,0:T(1,128)} %k_gain.1, bf16[128,3072]{1,0:T(8,128)(2,1)} %w_out.1), custom_call_target="tpu_custom_call" | custom-call | flops 4000000000 | bytes 8000000 | tf_op jit(solution)/shard_map/pallas_call | solution.py:611
  79.4 0.7 copy.10

commit v2 on v0

--- a/solution.py
+++ b/solution.py
@@ -345,7 +345,6 @@
         tmp_out[hi] = mixed.reshape(slabs, tok, HEAD_DIM)
 
     lax.fori_loop(1, half, gather_step, 0)
-    temporal(z_hi)
     gather_step(half, 0)
     pass_slab.start()
     sp_in[me] = qkv[:, me]
@@ -354,6 +353,7 @@
 
     @pl.when(mine_late)
     def _():
+        temporal(z_hi)
         temporal(1 - z_hi)
 
     part_in = sp_in.at[0 : cols - 1]
@@ -393,6 +393,7 @@
 
     @pl.when(jnp.logical_not(mine_late))
     def _():
+        temporal(z_hi)
         temporal(1 - z_hi)
 
 

time: 79.9 us -> 79.9 us (level)
  no operation moved by 1% of the time
where the time goes in v2:
time: 79.9 us; the launch traced here: 79.8 us
  Pallas kernels  79.1 us (99%)
    pallas_call x1, Pallas kernels, body(): pl.pallas_call(functools.partial(kernel, ring, cols), out_shape=pltpu.VME...  79.1 us

profile of v2, /device:TPU:6, one launch (start us, length us, event | category | flops | bytes accessed | tf_op | source)
XLA Modules:
  0.0 79.8 jit_solution(396944095417613328)
XLA Ops:
  0.0 79.1 %shard_map.73 = bf16[2,16,3072]{2,1,0:T(8,128)(2,1)S(1)} custom-call(bf16[2,16,3072]{2,1,0:T(8,128)(2,1)} %bitcast.9, s32[2,16]{1,0:T(2,128)} %levels_in.1, bf16[3,48,3072]{2,1,0:T(8,128)(2,1)} %bitcast.8, bf16[3072,384]{1,0:T(8,128)(2,1)} %bitcast.7, f32[1,128]{1,0:T(1,128)} %q_gain.1, f32[1,128]{1,0:T(1,128)} %k_gain.1, bf16[128,3072]{1,0:T(8,128)(2,1)} %w_out.1), custom_call_target="tpu_custom_call" | custom-call | flops 4000000000 | bytes 8000000 | tf_op jit(solution)/shard_map/pallas_call | solution.py:612
  79.1 0.7 copy.10
